TPU v7x, 128 devices: a whole 4x4x4 slice. The times are simulated.
128 devices in a mesh: row: 16 (over z, y), col: 8 (over x, core).
Axes of the slice: x: 4, y: 4, z: 4, core: 2. Of those that a mesh axis runs over, the one named last changes fastest.
Arguments:
- matrix: float32 [2, 8192, 4, 4096], P(None, 'row', None, 'col'), may hold values from -10 to 14, as said below
- inverse_factors: float32 [2, 512, 512], replicated, may hold values from -0.05574408 to 0.05574408
Outputs:
- panels: float32 [2, 2, 8192, 512], P(None, None, 'row')
- updated: float32 [2, 8192, 4, 4096], P(None, 'row', None, 'col')
Inputs may be any that keep to these rules, and one draw needn't show every extreme that they name: Read as an 16384 x 16384 matrix, matrix is symmetric.
All inputs are finite; a program needn't handle non-finite values.
Results may differ from a plain program's by a relative error of at most 0.00012.
Values sent between devices are 32-bit elements; how exact they have to be, the bound alone decides.
No kernel may reach another device: no remote copies, remote signals or barrier semaphores. Data moves between devices by JAX's collectives and lax.ppermute only.
A program may use at most 128 MiB of HBM per device.

v0:
```python
import jax
import jax.numpy as jnp
from jax import lax
from jax.sharding import PartitionSpec as P


def from_root(x, axis, root):
    mine = lax.axis_index(axis) == root
    return lax.psum(jnp.where(mine, x, jnp.zeros_like(x)), axis)


def panel_rows(column, factor, row_blocks, step):
    product = jnp.einsum("anj,ij->ani", column, factor, precision=lax.Precision.HIGHEST)
    return jnp.where((row_blocks >= step)[:, None, None], product, 0.0)


def row_panel_of(current, factor, row_blocks, step, n_col):
    local = step // n_col
    result = from_root(
        panel_rows(current[:, :, local, :], factor, row_blocks, step), "col", step % n_col
    )
    return result


def column_panel(row_panel, ratio, n_col, pcol):
    pieces = [from_root(row_panel, "row", pcol + part * n_col) for part in range(ratio)]
    stacked = jnp.stack(pieces, axis=1)
    return stacked.reshape((-1,) + row_panel.shape[1:])


def trailing(row_panel, col_panel, row_blocks, col_blocks, step):
    update = jnp.einsum("ani,cmi->ancm", row_panel, col_panel, precision=lax.Precision.HIGHEST)
    mask = (row_blocks > step)[:, None, None, None] & (col_blocks > step)[None, None, :, None]
    return jnp.where(mask, update, 0.0)


def body(matrix, inverse_factors):
    rbd = matrix.shape[0]
    cbd = matrix.shape[2]
    n_row = lax.axis_size("row")
    n_col = lax.axis_size("col")
    ratio = n_row // n_col
    prow = lax.axis_index("row")
    pcol = lax.axis_index("col")
    row_blocks = jnp.arange(rbd, dtype=jnp.int32) * n_row + prow
    col_blocks = jnp.arange(cbd, dtype=jnp.int32) * n_col + pcol
    current = matrix
    panels = []
    for step in range(2):
        rows_now = row_panel_of(current, inverse_factors[step], row_blocks, step, n_col)
        cols_now = column_panel(rows_now, ratio, n_col, pcol)
        current = current - trailing(rows_now, cols_now, row_blocks, col_blocks, step)
        panels.append(rows_now)
    return (jnp.stack(panels), current)


def solution(mesh):
    placed = (P(None, "row", None, "col"), P())
    return jax.shard_map(
        body,
        mesh=mesh,
        in_specs=placed,
        out_specs=(P(None, None, "row", None), P(None, "row", None, "col")),
        check_vma=False,
    )
```

profile of v0, /device:TPU:1, one launch (start us, length us, event | category | flops | bytes accessed | tf_op | source)
XLA Modules:
  0.0 440.6 jit_solution(8666622533113412183)
XLA Ops:
  7.2 0.0 all-reduce.7.cloned.1.call-start
  7.2 0.0 slice-start.2
  7.2 1.6 slice-done.2
  8.8 6.0 %select_select_fusion.1 = f32[2,512,512]{2,1,0:T(8,128)} fusion(f32[2,512,1,512]{3,2,1,0:T(1,128)S(1)} %slice-done.2, f32[2,512,512]{2,1,0:T(8,128)} %param.3, pred[2]{0:T(512)(128)(4,1)S(1)} %broadcast_compare_fusion.3, pred[]{:T(512)S(6)} %eq.14), kind=kOutput, calls=%fused_computation.16 | convolution fusion | flops 3222274048 | bytes 5242883 | tf_op jit(solution)/shard_map/anj,ij->ani/dot_general | solution.py:13
  14.8 0.0 all-reduce.7.cloned.1.call-update
  14.9 0.0 all-reduce.13.cloned.1.call-start
  14.9 66.9 %all-reduce.7.cloned.1.call-done = f32[2,512,512]{2,1,0:T(8,128)} async-done(((f32[2,512,512]{2,1,0:T(8,128)}), f32[2,512,512]{2,1,0:T(8,128)}) %all-reduce.7.cloned.1.call-update) | async-done | bytes 2097168 | tf_op jit(solution)/shard_map/psum | solution.py:9
  81.9 4.3 select_bitcast_fusion.3
  86.2 0.0 all-reduce.13.cloned.1.call-update
  86.2 0.2 all-reduce.9.cloned.1.call-start
  86.4 0.1 broadcast_and_fusion.1
  86.5 104.9 %all-reduce.13.cloned.1.call-done = (f32[2,1,512,512]{3,2,0,1:T(8,128)}, f32[2,1,512,512]{3,2,0,1:T(8,128)}) async-done(((f32[2,1,512,512]{3,2,0,1:T(8,128)}, f32[2,1,512,512]{3,2,0,1:T(8,128)}), (f32[2,1,512,512]{3,2,0,1:T(8,128)}, f32[2,1,512,512]{3,2,0,1:T(8,128)})) %all-reduce.13.cloned.1.call-update) | async-done | bytes 4194320 | tf_op jit(solution)/shard_map/psum | solution.py:9
  191.4 2.7 pad_maximum_fusion
  194.1 0.0 copy-start.1
  194.1 0.4 copy.8
  194.6 1.1 copy-done.1
  195.7 0.0 copy-start.3
  195.7 22.8 %copy_subtract_fusion = f32[2,512,4,512]{3,1,2,0:T(8,128)S(1)} fusion(f32[2,512,4,512]{3,2,1,0:T(4,128)} %param.2, pred[2,4]{1,0:T(4,128)(4,1)S(1)} %broadcast_and_fusion.1, f32[4,512,512,1]{2,1,0,3:T(8,128)S(1)} %bitcast.51, f32[2,512,512]{2,1,0:T(8,128)S(1)} %copy-done.1), kind=kOutput, calls=%fused_computation | convolution fusion | flops 12889096192 | bytes 23068680 | tf_op jit(solution)/shard_map/ani,cmi->ancm/dot_general | solution.py:32
  218.5 0.0 copy-start
  218.5 3.4 copy-done
  221.9 0.0 copy-done.3
  221.9 4.8 %select_select_fusion = f32[2,512,512]{2,1,0:T(8,128)} fusion(f32[2,512,4,512]{3,1,2,0:T(8,128)S(1)} %copy_subtract_fusion, f32[2,512,512]{2,1,0:T(8,128)S(1)} %copy-done.3, pred[2]{0:T(512)(128)(4,1)S(1)} %get-tuple-element.14, pred[]{:T(512)S(6)} %eq.15), kind=kOutput, calls=%fused_computation.13 | convolution fusion | flops 3222274048 | bytes 5243393 | tf_op jit(solution)/shard_map/anj,ij->ani/dot_general | solution.py:13
  226.7 0.0 all-reduce.9.cloned.1.call-update
  226.7 0.0 all-reduce.11.cloned.1.call-start
  226.7 63.6 %all-reduce.9.cloned.1.call-done = f32[2,512,512]{2,1,0:T(8,128)} async-done(((f32[2,512,512]{2,1,0:T(8,128)}), f32[2,512,512]{2,1,0:T(8,128)}) %all-reduce.9.cloned.1.call-update) | async-done | bytes 2097168 | tf_op jit(solution)/shard_map/psum | solution.py:9
  290.4 4.3 select_bitcast_fusion.1
  294.7 0.0 all-reduce.11.cloned.1.call-update
  294.8 0.1 broadcast_and_fusion
  294.8 4.2 pad_maximum_fusion.1
  299.1 100.9 %all-reduce.11.cloned.1.call-done = (f32[2,1,512,512]{3,2,0,1:T(8,128)}, f32[2,1,512,512]{3,2,0,1:T(8,128)}) async-done(((f32[2,1,512,512]{3,2,0,1:T(8,128)}, f32[2,1,512,512]{3,2,0,1:T(8,128)}), (f32[2,1,512,512]{3,2,0,1:T(8,128)}, f32[2,1,512,512]{3,2,0,1:T(8,128)})) %all-reduce.11.cloned.1.call-update) | async-done | bytes 4194320 | tf_op jit(solution)/shard_map/psum | solution.py:9
  400.0 0.0 slice-start
  400.0 2.8 pad_maximum_fusion.2
  402.8 0.0 slice-start.1
  402.8 0.0 copy-start.2
  402.9 0.4 copy.10
  403.3 0.1 slice-done
  403.4 1.7 slice-done.1
  405.2 0.6 copy-done.2
  405.8 16.1 %select_subtract_fusion = f32[2,512,4,512]{3,1,2,0:T(8,128)} fusion(f32[2,512,4,512]{3,1,2,0:T(8,128)S(1)} %bitcast.47, pred[2,4]{1,0:T(4,128)(4,1)S(1)} %broadcast_and_fusion, f32[4,512,512,1]{2,1,0,3:T(8,128)S(1)} %bitcast.48, f32[2,512,512]{2,1,0:T(8,128)S(1)} %copy-done.2), kind=kOutput, calls=%fused_computation.1 | convolution fusion | flops 12889096192 | bytes 23068680 | tf_op jit(solution)/shard_map/ani,cmi->ancm/dot_general | solution.py:32
  421.9 12.2 %copy.11 = f32[2,512,4,512]{3,2,1,0:T(4,128)} copy(f32[2,512,4,512]{3,1,2,0:T(8,128)} %select_subtract_fusion) | data formatting | bytes 16777216
  (6 shorter events, 0.0 us)
Async XLA Ops:
  7.2 74.7 %all-reduce.7.cloned.1.call-start = ((), (), s32[]{:S(2)}) async-start(), calls=%async_computation | async-start | bytes 4194304 | tf_op jit(solution)/shard_map/psum | solution.py:9
  7.2 1.6 slice-start.2
  14.9 176.6 %all-reduce.13.cloned.1.call-start = ((), (), s32[]{:S(2)}) async-start(), calls=%async_computation.3 | async-start | bytes 8388608 | tf_op jit(solution)/shard_map/psum | solution.py:9
  86.2 204.2 %all-reduce.9.cloned.1.call-start = ((), (), s32[]{:S(2)}) async-start(), calls=%async_computation.1 | async-start | bytes 4194304 | tf_op jit(solution)/shard_map/psum | solution.py:9
  194.1 1.6 copy-start.1
  195.7 26.2 %copy-start.3 = (f32[2,512,512]{2,1,0:T(8,128)S(1)}, f32[2,512,512]{2,1,0:T(8,128)}, u32[]{:S(2)}) copy-start(f32[2,512,512]{2,1,0:T(8,128)} %param.3) | copy-start | bytes 6291460
  218.5 3.4 copy-start
  226.7 173.3 %all-reduce.11.cloned.1.call-start = ((), (), s32[]{:S(2)}) async-start(), calls=%async_computation.2 | async-start | bytes 8388608 | tf_op jit(solution)/shard_map/psum | solution.py:9
  400.0 3.4 slice-start
  402.8 2.3 slice-start.1
  402.8 2.9 copy-start.2
Sparse Core Ops, SparseCore 0:
  15.0 66.8 all-reduce.6
  86.3 105.0 all-reduce.12
  226.8 63.5 all-reduce.8
  294.9 105.0 all-reduce.10
where the time goes:
time: 441 us
  waiting for transfers between devices  336 us (76%)
  matrix products  49.7 us (11%)
  local copies, waits for them, and re-layouts  21.6 us (5%)
  other arithmetic  18.6 us (4%)
  between operations  13.9 us (3%)
    psum x4, waiting for transfers between devices, from_root(): return lax.psum(jnp.where(mine, x, jnp.zeros_like(x)), axis)  336 us
    dot_general x2, matrix products, trailing(): jnp.einsum('ani,cmi->ancm', row_panel, col_panel, precision=lax.Precision...  38.9 us
    unnamed x13, local copies, waits for them, and re-layouts  19.2 us
    another operation x4, other arithmetic, column_panel(): stacked = jnp.stack(pieces, axis=1)  14.1 us
    dot_general x2, matrix products, panel_rows(): jnp.einsum('anj,ij->ani', column, factor, precision=lax.Precision.HIGHEST)  10.8 us
  transfers between devices with their start and end apart: 4, of which 4 were waited for; matrix products, arithmetic and copies ran while one was open for 1% of the time, Pallas kernels for 0%

commit v1 on v0

--- a/solution.py
+++ b/solution.py
@@ -6,7 +6,7 @@
 
 def from_root(x, axis, root):
     mine = lax.axis_index(axis) == root
-    return lax.psum(jnp.where(mine, x, jnp.zeros_like(x)), axis)
+    return jnp.sum(lax.all_gather(jnp.where(mine, x, jnp.zeros_like(x)), axis), axis=0)
 
 
 def panel_rows(column, factor, row_blocks, step):

time: 441 us -> 1110 us (2.52)
  waiting for transfers between devices: 336 us -> 934 us
  other arithmetic: 18.6 us -> 90 us
    all_gather x0 -> x6, waiting for transfers between devices: none -> 933 us  [from_root(): lax.all_gather(jnp.where(mine, x, jnp.zeros_like(x)), axis)]
    psum x4 -> x0, waiting for transfers between devices: 336 us -> none  [from_root(): return lax.psum(jnp.where(mine, x, jnp.zeros_like(x)), axis)]
    reduce_sum x0 -> x6, other arithmetic: none -> 73.5 us  [from_root(): jnp.sum(lax.all_gather(jnp.where(mine, x, jnp.zeros_like(x)), axis), axis=0)]
  transfers between devices with their start and end apart: 4 -> 6, of which waited for: 4 -> 6; matrix products, arithmetic and copies ran while one was open for 1% -> 3% of each run, Pallas kernels for 0% -> 0%
where the time goes in v1:
time: 1110 us
  waiting for transfers between devices  934 us (84%)
  other arithmetic  90 us (8%)
  matrix products  51.1 us (5%)
  local copies, waits for them, and re-layouts  17.2 us (2%)
  between operations  14.5 us (1%)
    all_gather x6, waiting for transfers between devices, from_root(): lax.all_gather(jnp.where(mine, x, jnp.zeros_like(x)), axis)  933 us
    reduce_sum x6, other arithmetic, from_root(): jnp.sum(lax.all_gather(jnp.where(mine, x, jnp.zeros_like(x)), axis), axis=0)  73.5 us
    dot_general x2, matrix products, trailing(): jnp.einsum('ani,cmi->ancm', row_panel, col_panel, precision=lax.Precision...  40.3 us
  transfers between devices with their start and end apart: 6, of which 6 were waited for; matrix products, arithmetic and copies ran while one was open for 3% of the time, Pallas kernels for 0%

profile of v1, /device:TPU:1, one launch (start us, length us, event | category | flops | bytes accessed | tf_op | source)
XLA Modules:
  0.0 1107.8 jit_solution(17835467254643155724)
XLA Ops:
  7.2 0.0 all-gather.17.cloned.1.call-start
  7.2 0.0 slice-start
  7.2 1.6 slice-done
  8.8 6.0 select_select_fusion.1
  14.8 0.0 all-gather.17.cloned.1.call-update
  14.9 0.0 all-gather.9.cloned.1.call-start
  14.9 88.7 %all-gather.17.cloned.1.call-done = f32[16,512,512]{2,1,0:T(8,128)} async-done(((f32[2,512,512]{2,1,0:T(8,128)}), f32[16,512,512]{2,1,0:T(8,128)}) %all-gather.17.cloned.1.call-update) | async-done | bytes 16777232 | tf_op jit(solution)/shard_map/all_gather | solution.py:9
  103.6 8.1 reduce_sum.54
  111.7 2.7 broadcast_select_fusion.3
  114.4 0.0 all-gather.9.cloned.1.call-update
  114.4 0.0 all-gather.11.cloned.1.call-start
  114.5 0.7 all-gather.11.cloned.1.call-update
  115.2 0.5 all-gather.19.cloned.1.call-start
  115.7 0.1 broadcast_and_fusion.1
  115.8 196.2 %all-gather.9.cloned.1.call-done = f32[16,2,512,512]{3,2,1,0:T(8,128)} async-done(((f32[1,2,512,512]{3,2,1,0:T(8,128)}), f32[16,2,512,512]{3,2,1,0:T(8,128)}) %all-gather.9.cloned.1.call-update) | async-done | bytes 33554448 | tf_op jit(solution)/shard_map/all_gather | solution.py:9
  312.0 14.2 %reduce_sum.55 = f32[2,512,512]{2,1,0:T(8,128)} reduce(f32[16,2,512,512]{3,2,1,0:T(8,128)} %all-gather.9.cloned.1.call-done, f32[]{:T(128)} %constant.13.clone.1), dimensions={0}, to_apply=%region_1.2 | reduce | flops 7864320 | bytes 35651588 | tf_op jit(solution)/shard_map/reduce_sum | solution.py:9
  326.2 185.3 %all-gather.11.cloned.1.call-done = f32[16,2,512,512]{3,2,1,0:T(8,128)} async-done(((f32[1,2,512,512]{3,2,1,0:T(8,128)}), f32[16,2,512,512]{3,2,1,0:T(8,128)}) %all-gather.11.cloned.1.call-update) | async-done | bytes 33554448 | tf_op jit(solution)/shard_map/all_gather | solution.py:9
  511.6 14.1 %reduce_sum.56 = f32[2,512,512]{2,1,0:T(8,128)} reduce(f32[16,2,512,512]{3,2,1,0:T(8,128)} %all-gather.11.cloned.1.call-done, f32[]{:T(128)} %constant.13.clone.1), dimensions={0}, to_apply=%region_2.3 | reduce | flops 7864320 | bytes 35651588 | tf_op jit(solution)/shard_map/reduce_sum | solution.py:9
  525.6 2.7 pad_maximum_fusion
  528.3 0.0 copy-start.2
  528.3 22.7 %copy_subtract_fusion = f32[2,512,4,512]{3,1,2,0:T(8,128)S(1)} fusion(f32[2,512,4,512]{3,2,1,0:T(4,128)} %param.2, pred[2,4]{1,0:T(4,128)(4,1)S(1)} %broadcast_and_fusion.1, f32[4,512,512,1]{2,1,0,3:T(8,128)S(1)} %bitcast.53, f32[2,512,512]{2,1,0:T(8,128)S(1)} %reduce_sum.54), kind=kOutput, calls=%fused_computation | convolution fusion | flops 12889096192 | bytes 23068680 | tf_op jit(solution)/shard_map/ani,cmi->ancm/dot_general | solution.py:32
  551.0 0.0 copy-start
  551.0 3.4 copy-done
  554.4 0.0 copy-done.2
  554.4 4.8 select_select_fusion
  559.2 0.0 all-gather.19.cloned.1.call-update
  559.2 0.0 all-gather.13.cloned.1.call-start
  559.3 85.1 %all-gather.19.cloned.1.call-done = f32[16,512,512]{2,1,0:T(8,128)} async-done(((f32[2,512,512]{2,1,0:T(8,128)}), f32[16,512,512]{2,1,0:T(8,128)}) %all-gather.19.cloned.1.call-update) | async-done | bytes 16777232 | tf_op jit(solution)/shard_map/all_gather | solution.py:9
  644.4 9.4 reduce_sum.57
  653.8 4.3 broadcast_select_fusion.1
  658.1 0.0 all-gather.13.cloned.1.call-update
  658.1 0.0 all-gather.15.cloned.1.call-start
  658.2 0.5 all-gather.15.cloned.1.call-update
  658.7 0.1 broadcast_and_fusion
  658.8 4.2 pad_maximum_fusion.1
  663.1 192.6 %all-gather.13.cloned.1.call-done = f32[16,2,512,512]{3,2,1,0:T(8,128)} async-done(((f32[1,2,512,512]{3,2,1,0:T(8,128)}), f32[16,2,512,512]{3,2,1,0:T(8,128)}) %all-gather.13.cloned.1.call-update) | async-done | bytes 33554448 | tf_op jit(solution)/shard_map/all_gather | solution.py:9
  855.7 13.6 %reduce_sum.58 = f32[2,512,512]{2,1,0:T(8,128)S(1)} reduce(f32[16,2,512,512]{3,2,1,0:T(8,128)} %all-gather.13.cloned.1.call-done, f32[]{:T(128)} %constant.13.clone.1), dimensions={0}, to_apply=%region_4.5 | reduce | flops 7864320 | bytes 35651588 | tf_op jit(solution)/shard_map/reduce_sum | solution.py:9
  869.3 185.2 %all-gather.15.cloned.1.call-done = f32[16,2,512,512]{3,2,1,0:T(8,128)} async-done(((f32[1,2,512,512]{3,2,1,0:T(8,128)}), f32[16,2,512,512]{3,2,1,0:T(8,128)}) %all-gather.15.cloned.1.call-update) | async-done | bytes 33554448 | tf_op jit(solution)/shard_map/all_gather | solution.py:9
  1054.6 14.1 %reduce_sum.59 = f32[2,512,512]{2,1,0:T(8,128)} reduce(f32[16,2,512,512]{3,2,1,0:T(8,128)} %all-gather.15.cloned.1.call-done, f32[]{:T(128)} %constant.13.clone.1), dimensions={0}, to_apply=%region_5.6 | reduce | flops 7864320 | bytes 35651588 | tf_op jit(solution)/shard_map/reduce_sum | solution.py:9
  1068.6 0.0 copy-start.1
  1068.6 2.3 pad_maximum_fusion.2
  1071.0 0.0 copy-done.1
  1071.0 17.5 %select_subtract_fusion = f32[2,512,4,512]{3,1,2,0:T(8,128)} fusion(f32[2,512,4,512]{3,1,2,0:T(8,128)} %copy-done, pred[2,4]{1,0:T(4,128)(4,1)S(1)} %broadcast_and_fusion, f32[4,512,512,1]{2,1,0,3:T(8,128)S(1)} %bitcast.50, f32[2,512,512]{2,1,0:T(8,128)S(1)} %copy-done.1), kind=kOutput, calls=%fused_computation.1 | convolution fusion | flops 12889096192 | bytes 23068680 | tf_op jit(solution)/shard_map/ani,cmi->ancm/dot_general | solution.py:32
  1088.6 12.2 %copy.9 = f32[2,512,4,512]{3,2,1,0:T(4,128)} copy(f32[2,512,4,512]{3,1,2,0:T(8,128)} %select_subtract_fusion) | data formatting | bytes 16777216
  (5 shorter events, 0.0 us)
Async XLA Ops:
  7.2 96.4 %all-gather.17.cloned.1.call-start = ((), (), s32[]{:S(2)}) async-start(), calls=%async_computation.4 | async-start | bytes 18874368 | tf_op jit(solution)/shard_map/all_gather | solution.py:9
  7.2 1.6 slice-start
  14.9 297.1 %all-gather.9.cloned.1.call-start = ((), (), s32[]{:S(2)}) async-start(), calls=%async_computation | async-start | bytes 35651584 | tf_op jit(solution)/shard_map/all_gather | solution.py:9
  114.4 397.1 %all-gather.11.cloned.1.call-start = ((), (), s32[]{:S(2)}) async-start(), calls=%async_computation.1 | async-start | bytes 35651584 | tf_op jit(solution)/shard_map/all_gather | solution.py:9
  115.2 529.2 %all-gather.19.cloned.1.call-start = ((), (), s32[]{:S(2)}) async-start(), calls=%async_computation.5 | async-start | bytes 18874368 | tf_op jit(solution)/shard_map/all_gather | solution.py:9
  528.3 26.1 %copy-start.2 = (f32[2,512,512]{2,1,0:T(8,128)S(1)}, f32[2,512,512]{2,1,0:T(8,128)}, u32[]{:S(2)}) copy-start(f32[2,512,512]{2,1,0:T(8,128)} %param.3) | copy-start | bytes 6291460
  551.0 3.4 copy-start
  559.2 296.5 %all-gather.13.cloned.1.call-start = ((), (), s32[]{:S(2)}) async-start(), calls=%async_computation.2 | async-start | bytes 35651584 | tf_op jit(solution)/shard_map/all_gather | solution.py:9
  658.1 396.4 %all-gather.15.cloned.1.call-start = ((), (), s32[]{:S(2)}) async-start(), calls=%async_computation.3 | async-start | bytes 35651584 | tf_op jit(solution)/shard_map/all_gather | solution.py:9
  1068.6 2.4 copy-start.1
Sparse Core Ops, SparseCore 0:
  15.0 88.5 all-gather.16
  114.5 197.3 all-gather.8
  314.7 196.8 all-gather.10
  559.4 84.9 all-gather.18
  658.3 197.3 all-gather.12
  857.7 196.8 all-gather.14
